TPU v7x, 256 devices: a whole 4x4x8 slice. The times are simulated.
256 devices in a mesh: seq: 32 (over y, z), head: 8 (over x, core).
Axes of the slice: x: 4, y: 4, z: 8, core: 2. Of those that a mesh axis runs over, the one named last changes fastest.
Arguments:
- queries: bfloat16 [32768, 4096], P(('seq', 'head')), may hold values from -8 to 8
- key_heads: bfloat16 [32768, 1024], P('seq', 'head'), may hold values from -8 to 8
- value_heads: bfloat16 [32768, 1024], P('seq', 'head'), may hold values from -6 to 6
- output_grad: bfloat16 [32768, 4096], P(('seq', 'head')), may hold values from -6 to 6
- doc_starts: int32 [32], replicated, may hold values from 0 to 32000, as said below
Outputs:
- attended: bfloat16 [32768, 4096], P(('seq', 'head'))
- query_grad: bfloat16 [32768, 4096], P(('seq', 'head'))
- key_grad: bfloat16 [32768, 1024], P('seq', 'head')
- value_grad: bfloat16 [32768, 1024], P('seq', 'head')
Inputs may be any that keep to these rules, and one draw needn't show every extreme that they name: doc_starts[0] is 0 and the starts increase; every document has between half of 1024 and 1536 tokens, a multiple of 128, and the documents fill all 32768 tokens; some document has exactly 1536 tokens.
All inputs are finite; a program needn't handle non-finite values.
Results may differ from a plain program's by a relative error of at most 0.012.
The roundings to bfloat16 on the way count: a program that leaves them out, or rounds other values in their place, can miss the bound.
Values may be sent and summed in bfloat16 or wider, within the bound.
A program may use at most 64 MiB of HBM per device.

v0:
```python
import jax
import jax.numpy as jnp
from jax import lax
from jax.sharding import PartitionSpec as P

HEAD = 128
QH = 32
KVH = 8


def from_behind(value, axis, by):
    count = lax.axis_size(axis)
    pairs = [(i, i + by) for i in range(count) if 0 <= i + by < count]
    return lax.ppermute(value, axis, pairs)


def doc_of(positions, doc_starts):
    passed = (positions[:, None] >= doc_starts[None, :]).astype(jnp.int32)
    return jnp.sum(passed, axis=1) - 1


def masked_scores(q_tile, k_tile, q_doc, k_doc, q_pos, k_pos, factor):
    products = (
        jnp.einsum("qgjd,kgd->gjqk", q_tile, k_tile, preferred_element_type=jnp.float32) * factor
    )
    allowed = (q_doc[:, None] == k_doc[None, :]) & (k_pos[None, :] <= q_pos[:, None])
    return jnp.where(allowed[None, None], products, -jnp.inf)


def local(queries, key_heads, value_heads, output_grad, doc_starts):
    shard_rows = key_heads.shape[0]
    kv_local = key_heads.shape[1] // HEAD
    group_size = QH // KVH
    factor = HEAD ** (-0.5)
    half_rows = shard_rows // 2
    block_rows = min(512, half_rows)
    q_blocks = shard_rows // block_rows
    win_rows = half_rows + 2 * shard_rows
    k_blocks = win_rows // block_rows
    q_own = lax.all_to_all(queries, "head", split_axis=1, concat_axis=0, tiled=True)
    near_keys, near_values = from_behind((key_heads, value_heads), "seq", 1)
    far_keys, far_values = from_behind((key_heads[half_rows:], value_heads[half_rows:]), "seq", 2)
    win_keys = jnp.concatenate([far_keys, near_keys, key_heads], 0).reshape(
        win_rows, kv_local, HEAD
    )
    win_values = jnp.concatenate([far_values, near_values, value_heads], 0).reshape(
        win_rows, kv_local, HEAD
    )
    anchor = lax.axis_index("seq") * shard_rows
    win_pos = anchor - shard_rows - half_rows + jnp.arange(win_rows, dtype=jnp.int32)
    win_doc = doc_of(win_pos, doc_starts)
    own_pos = anchor + jnp.arange(shard_rows, dtype=jnp.int32)
    own_doc = doc_of(own_pos, doc_starts)
    q_heads = q_own.reshape(shard_rows, kv_local, group_size, HEAD)
    stat_shape = (kv_local, group_size, block_rows)

    def needed(row_start, col_start):
        reaches = win_pos[col_start] <= own_pos[row_start + block_rows - 1]
        return reaches & (win_doc[col_start + block_rows - 1] >= own_doc[row_start])

    def query_tile(row_start):
        return (
            lax.dynamic_slice_in_dim(q_heads, row_start, block_rows, 0),
            lax.dynamic_slice_in_dim(own_doc, row_start, block_rows, 0),
            lax.dynamic_slice_in_dim(own_pos, row_start, block_rows, 0),
        )

    def key_tile(col_start):
        return (
            lax.dynamic_slice_in_dim(win_keys, col_start, block_rows, 0),
            lax.dynamic_slice_in_dim(win_values, col_start, block_rows, 0),
            lax.dynamic_slice_in_dim(win_doc, col_start, block_rows, 0),
            lax.dynamic_slice_in_dim(win_pos, col_start, block_rows, 0),
        )

    def forward_block(number):
        row_start = number * block_rows
        q_tile, q_doc, q_pos = query_tile(row_start)

        def stats_step(column, current):
            col_start = column * block_rows

            def stats_compute(holding):
                run_max, run_sum = holding
                k_tile, v_tile, k_doc, k_pos = key_tile(col_start)
                scores = masked_scores(q_tile, k_tile, q_doc, k_doc, q_pos, k_pos, factor)
                new_max = jnp.maximum(run_max, jnp.max(scores, axis=-1))
                run_sum = run_sum * jnp.exp(run_max - new_max) + jnp.sum(
                    jnp.exp(scores - new_max[..., None]), axis=-1
                )
                return (new_max, run_sum)

            return lax.cond(
                needed(row_start, col_start), stats_compute, lambda holding: holding, current
            )

        run_max, run_sum = lax.fori_loop(
            0,
            k_blocks,
            stats_step,
            (jnp.full(stat_shape, -1e30, jnp.float32), jnp.zeros(stat_shape, jnp.float32)),
        )
        log_total = run_max + jnp.log(run_sum)

        def value_step(column, current):
            col_start = column * block_rows

            def value_compute(partial_value):
                k_tile, v_tile, k_doc, k_pos = key_tile(col_start)
                scores = masked_scores(q_tile, k_tile, q_doc, k_doc, q_pos, k_pos, factor)
                weights = jnp.exp(scores - log_total[..., None]).astype(jnp.bfloat16)
                return partial_value + jnp.einsum(
                    "gjqk,kgd->gjqd", weights, v_tile, preferred_element_type=jnp.float32
                )

            return lax.cond(
                needed(row_start, col_start),
                value_compute,
                lambda partial_value: partial_value,
                current,
            )

        partial_value = lax.fori_loop(
            0,
            k_blocks,
            value_step,
            jnp.zeros((kv_local, group_size, block_rows, HEAD), jnp.float32),
        )
        out_tile = (
            partial_value.astype(jnp.bfloat16)
            .transpose(2, 0, 1, 3)
            .reshape(block_rows, kv_local * group_size * HEAD)
        )
        return (out_tile, log_total)

    out_blocks, log_blocks = lax.map(forward_block, jnp.arange(q_blocks, dtype=jnp.int32))
    out_own = out_blocks.reshape(shard_rows, kv_local * group_size * HEAD)
    attended = lax.all_to_all(out_own, "head", split_axis=0, concat_axis=1, tiled=True)
    g_own = lax.all_to_all(output_grad, "head", split_axis=1, concat_axis=0, tiled=True)
    g_heads = g_own.reshape(shard_rows, kv_local, group_size, HEAD)
    row_delta = jnp.sum(
        g_heads.astype(jnp.float32)
        * out_own.reshape(shard_rows, kv_local, group_size, HEAD).astype(jnp.float32),
        axis=-1,
    )

    def backward_block(carried, number):
        key_acc, value_acc = carried
        row_start = number * block_rows
        q_tile, q_doc, q_pos = query_tile(row_start)
        g_tile = lax.dynamic_slice_in_dim(g_heads, row_start, block_rows, 0)
        log_tile = log_blocks[number]
        delta_tile = lax.dynamic_slice_in_dim(row_delta, row_start, block_rows, 0).transpose(
            1, 2, 0
        )

        def grad_step(column, current):
            col_start = column * block_rows

            def grad_compute(holding):
                q_acc, k_acc, v_acc = holding
                k_tile, v_tile, k_doc, k_pos = key_tile(col_start)
                scores = masked_scores(q_tile, k_tile, q_doc, k_doc, q_pos, k_pos, factor)
                exact = jnp.exp(scores - log_tile[..., None])
                weights = exact.astype(jnp.bfloat16)
                d_prob = jnp.einsum(
                    "qgjd,kgd->gjqk", g_tile, v_tile, preferred_element_type=jnp.float32
                )
                d_score = (exact * (d_prob - delta_tile[..., None])).astype(jnp.bfloat16)
                q_acc = q_acc + jnp.einsum(
                    "gjqk,kgd->gjqd", d_score, k_tile, preferred_element_type=jnp.float32
                )
                k_part = jnp.einsum(
                    "gjqk,qgjd->kgd", d_score, q_tile, preferred_element_type=jnp.float32
                )
                v_part = jnp.einsum(
                    "gjqk,qgjd->kgd", weights, g_tile, preferred_element_type=jnp.float32
                )
                k_acc = lax.dynamic_update_slice_in_dim(
                    k_acc,
                    lax.dynamic_slice_in_dim(k_acc, col_start, block_rows, 0) + k_part,
                    col_start,
                    0,
                )
                v_acc = lax.dynamic_update_slice_in_dim(
                    v_acc,
                    lax.dynamic_slice_in_dim(v_acc, col_start, block_rows, 0) + v_part,
                    col_start,
                    0,
                )
                return (q_acc, k_acc, v_acc)

            return lax.cond(
                needed(row_start, col_start), grad_compute, lambda holding: holding, current
            )

        q_start = jnp.zeros((kv_local, group_size, block_rows, HEAD), jnp.float32)
        q_acc, key_acc, value_acc = lax.fori_loop(
            0, k_blocks, grad_step, (q_start, key_acc, value_acc)
        )
        dq_tile = (
            (q_acc * factor)
            .astype(jnp.bfloat16)
            .transpose(2, 0, 1, 3)
            .reshape(block_rows, kv_local * group_size * HEAD)
        )
        return ((key_acc, value_acc), dq_tile)

    win_zeros = jnp.zeros((win_rows, kv_local, HEAD), jnp.float32)
    (key_acc, value_acc), dq_blocks = lax.scan(
        backward_block, (win_zeros, win_zeros), jnp.arange(q_blocks, dtype=jnp.int32)
    )
    key_acc = key_acc.reshape(win_rows, kv_local * HEAD)
    value_acc = value_acc.reshape(win_rows, kv_local * HEAD)
    far_pair = (key_acc[:half_rows], value_acc[:half_rows])
    near_key = key_acc[half_rows : half_rows + shard_rows]
    near_value = value_acc[half_rows : half_rows + shard_rows]
    from_near = (
        from_behind(near_key.astype(jnp.bfloat16), "seq", -1).astype(near_key.dtype),
        from_behind(near_value.astype(jnp.bfloat16), "seq", -1).astype(near_value.dtype),
    )
    key_total = key_acc[half_rows + shard_rows :] + from_near[0]
    value_total = value_acc[half_rows + shard_rows :] + from_near[1]
    from_far = (
        from_behind(far_pair[0].astype(jnp.bfloat16), "seq", -2).astype(jnp.float32),
        from_behind(far_pair[1].astype(jnp.bfloat16), "seq", -2).astype(jnp.float32),
    )
    key_total = key_total.at[half_rows:].add(from_far[0])
    value_total = value_total.at[half_rows:].add(from_far[1])
    key_grad = (key_total * factor).astype(jnp.bfloat16)
    value_grad = value_total.astype(jnp.bfloat16)
    dq_own = dq_blocks.reshape(shard_rows, kv_local * group_size * HEAD)
    query_grad = lax.all_to_all(dq_own, "head", split_axis=0, concat_axis=1, tiled=True)
    return (attended, query_grad, key_grad, value_grad)


def solution(mesh):
    return jax.shard_map(
        local,
        mesh=mesh,
        in_specs=(
            P(("seq", "head"), None),
            P("seq", "head"),
            P("seq", "head"),
            P(("seq", "head"), None),
            P(),
        ),
        out_specs=(
            P(("seq", "head"), None),
            P(("seq", "head"), None),
            P("seq", "head"),
            P("seq", "head"),
        ),
        check_vma=False,
    )
```

profile of v0, /device:TPU:8, one launch (start us, length us, event | category | flops | bytes accessed | tf_op | source)
XLA Modules:
  0.0 364.0 jit_solution(6334316828624399086)
XLA Ops:
  0.7 2.4 copy.59
  3.0 4.3 %all-to-all-start = ((bf16[128,8,512]{0,2,1:T(8,128)(2,1)}), bf16[128,8,512]{0,2,1:T(8,128)(2,1)S(1)}, u32[]{:S(2)}, u32[]{:S(2)}) async-start(bf16[128,8,512]{0,2,1:T(8,128)(2,1)} %bitcast.44), calls=%async_computation | async-start | bytes 2097152 | tf_op jit(solution)/shard_map/all_to_all | solution.py:40
  7.4 3.8 %collective-permute-start.3 = (bf16[1024,128]{1,0:T(8,128)(2,1)S(1)}, bf16[1024,128]{1,0:T(8,128)(2,1)S(1)}, u32[]{:S(2)}, u32[]{:S(2)}) collective-permute-start(bf16[1024,128]{1,0:T(8,128)(2,1)S(1)} %copy-done.3), channel_id=1, source_target_pairs={{0,8},{8,16},{16,24},{24,32},{32,40},{40,48},{48,56},{56,64},{64,7... | collective-permute-start | bytes 786440 | tf_op jit(solution)/shard_map/ppermute | solution.py:14
  11.9 5.2 %collective-permute-start.2 = (bf16[512,128]{1,0:T(8,128)(2,1)}, bf16[512,128]{1,0:T(8,128)(2,1)}, u32[]{:S(2)}, u32[]{:S(2)}) collective-permute-start(bf16[512,128]{1,0:T(8,128)(2,1)} %slice.77), channel_id=1, source_target_pairs={{0,16},{8,24},{16,32},{24,40},{32,48},{40,56},{48,64},{56,72},{64,... | collective-permute-start | bytes 393224 | tf_op jit(solution)/shard_map/ppermute | solution.py:14
  17.0 5.0 %collective-permute-start.1 = (bf16[1024,128]{1,0:T(8,128)(2,1)S(1)}, bf16[1024,128]{1,0:T(8,128)(2,1)}, u32[]{:S(2)}, u32[]{:S(2)}) collective-permute-start(bf16[1024,128]{1,0:T(8,128)(2,1)S(1)} %copy-done.2), channel_id=1, source_target_pairs={{0,8},{8,16},{16,24},{24,32},{32,40},{40,48},{48,56},{56,64},{64,7... | collective-permute-start | bytes 786440 | tf_op jit(solution)/shard_map/ppermute | solution.py:14
  22.1 3.4 collective-permute-start
  27.1 4.8 %all-to-all-start.2 = ((bf16[128,8,512]{0,2,1:T(8,128)(2,1)}), bf16[128,8,512]{0,2,1:T(8,128)(2,1)S(1)}, u32[]{:S(2)}, u32[]{:S(2)}) async-start(bf16[128,8,512]{0,2,1:T(8,128)(2,1)} %bitcast.51), calls=%async_computation.2 | async-start | bytes 2097152 | tf_op jit(solution)/shard_map/all_to_all | solution.py:139
  32.5 5.3 %collective-permute-done = bf16[512,128]{1,0:T(8,128)(2,1)S(1)} collective-permute-done((bf16[512,128]{1,0:T(8,128)(2,1)S(1)}, bf16[512,128]{1,0:T(8,128)(2,1)S(1)}, u32[]{:S(2)}, u32[]{:S(2)}) %collective-permute-start) | collective-permute-done | bytes 131104 | tf_op jit(solution)/shard_map/ppermute | solution.py:14
  39.5 1.8 maximum_bitcast_fusion.1
  45.8 2.1 all-to-all-done.2
  50.9 127.3 %while.153 = (s32[]{:T(128)}, bf16[2,512,512]{2,1,0:T(8,128)(2,1)}, f32[2,1,4,512]{3,2,1,0:T(4,128)}, s32[2]{0:T(128)S(1)}, bf16[1024,1,4,128]{3,0,2,1:T(8,128)(...) while((s32[]{:T(128)}, bf16[2,512,512]{2,1,0:T(8,128)(2,1)}, ...), condition=%wide.region_13.14_spmd.clone, body=%wide.region_2.13_spmd.clone.sunk | while | flops 818946560 | bytes 20271712 | solution.py:136
  56.1 29.2 %while.156 = (s32[]{:T(128)}, f32[1,4,512]{2,1,0:T(4,128)S(1)}, f32[1,4,512]{2,1,0:T(4,128)S(1)}, s32[2560]{0:T(1024)S(1)}, s32[1]{0:T(128)}, /*index=5*/s32[256...) while((s32[]{:T(128)}, f32[1,4,512]{2,1,0:T(4,128)S(1)}, ...), condition=%wide.region_8.8_spmd, body=%wide.region_3.7_spmd.sunk | while | flops 276566016 | bytes 9953737 | solution.py:97
  60.1 2.3 conditional.7
  66.4 2.3 conditional.7
  72.7 2.3 conditional.7
  79.0 2.3 conditional.7
  86.0 32.5 %while.157 = (s32[]{:T(128)}, f32[1,4,512,128]{3,2,1,0:T(8,128)S(1)}, s32[2560]{0:T(1024)S(1)}, s32[1]{0:T(128)}, s32[2560]{0:T(1024)S(1)}, /*index=5*/s32[1]{0:...) while((s32[]{:T(128)}, ...), condition=%wide.region_12.12_spmd, body=%wide.region_9.11_spmd.sunk | while | flops 542113792 | bytes 3433909 | solution.py:123
  89.9 3.3 conditional.8
  90.3 2.8 fusion.18
  97.0 3.3 conditional.8
  97.5 2.8 fusion.18
  104.2 3.3 conditional.8
  104.6 2.8 fusion.18
  111.3 3.3 conditional.8
  111.8 2.8 fusion.18
  125.3 24.7 %while.156 = (s32[]{:T(128)}, f32[1,4,512]{2,1,0:T(4,128)S(1)}, f32[1,4,512]{2,1,0:T(4,128)S(1)}, s32[2560]{0:T(1024)S(1)}, s32[1]{0:T(128)}, /*index=5*/s32[256...) while((s32[]{:T(128)}, f32[1,4,512]{2,1,0:T(4,128)S(1)}, ...), condition=%wide.region_8.8_spmd, body=%wide.region_3.7_spmd.sunk | while | flops 276566016 | bytes 9953737 | solution.py:97
  141.4 2.3 conditional.7
  147.7 2.3 conditional.7
  150.6 26.0 %while.157 = (s32[]{:T(128)}, f32[1,4,512,128]{3,2,1,0:T(8,128)S(1)}, s32[2560]{0:T(1024)S(1)}, s32[1]{0:T(128)}, s32[2560]{0:T(1024)S(1)}, /*index=5*/s32[1]{0:...) while((s32[]{:T(128)}, ...), condition=%wide.region_12.12_spmd, body=%wide.region_9.11_spmd.sunk | while | flops 542113792 | bytes 3433909 | solution.py:123
  166.2 3.3 conditional.8
  166.7 2.8 fusion.18
  173.4 3.3 conditional.8
  173.8 2.8 fusion.18
  179.9 4.4 %all-to-all-start.1 = ((bf16[8,128,512]{2,1,0:T(8,128)(2,1)}), bf16[8,128,512]{2,1,0:T(8,128)(2,1)}, u32[]{:S(2)}, u32[]{:S(2)}) async-start(bf16[8,128,512]{2,1,0:T(8,128)(2,1)} %bitcast.48), calls=%async_computation.1 | async-start | bytes 2097152 | tf_op jit(solution)/shard_map/all_to_all | solution.py:138
  184.4 1.9 copy.65
  186.2 2.8 multiply_reduce_fusion
  191.8 134.1 %while.155 = (s32[]{:T(128)}, f32[2560,1,128]{2,0,1:T(8,128)S(1)}, f32[2560,1,128]{2,0,1:T(8,128)}, bf16[2,512,512]{2,1,0:T(8,128)(2,1)}, s32[2]{0:T(128)}, /*in...) while((s32[]{:T(128)}, f32[2560,1,128]{2,0,1:T(8,128)S(1)}, ...), condition=%wide.region_20.21_spmd.clone, body=%wide.region_15.20_spmd.clone.sunk | while | flops 1354369536 | bytes 36498760 | solution.py:210
  206.1 61.0 %while.158 = (s32[]{:T(128)}, f32[1,4,512,128]{3,2,1,0:T(8,128)S(1)}, f32[2560,1,128]{2,0,1:T(8,128)S(1)}, f32[2560,1,128]{2,0,1:T(8,128)}, s32[2560]{0:T(1024)}...) while((s32[]{:T(128)}, ...), condition=%wide.region_19.19_spmd, body=%wide.region_16.18_spmd.sunk | while | flops 1353842688 | bytes 27501196 | solution.py:198
  210.4 9.8 %conditional.6 = ((f32[1,4,512,128]{3,2,1,0:T(8,128)S(1)}, f32[2560,1,128]{2,0,1:T(8,128)S(1)}, f32[2560,1,128]{2,0,1:T(8,128)})) conditional(s32[]{:T(128)} %bitcast.235, (f32[1,4,512,128]{3,2,1,0:T(8,128)S(1)}, f32[2560,1,128]{2,0,1:T(8,128)S(1)}, f32[2560,1,128]{2,0,1:T(8,128)}) %tuple.279, (s32[512]{0:T(512)}, s32[]{:T(128)}, ...), branch_computations={%region_17.16_spmd, %region_18.17_spmd} | conditional | flops 1353842688 | bytes 27500722 | solution.py:193
  213.3 2.9 fusion.67
  216.2 2.4 fusion.34
  224.6 9.8 %conditional.6 = ((f32[1,4,512,128]{3,2,1,0:T(8,128)S(1)}, f32[2560,1,128]{2,0,1:T(8,128)S(1)}, f32[2560,1,128]{2,0,1:T(8,128)})) conditional(s32[]{:T(128)} %bitcast.235, (f32[1,4,512,128]{3,2,1,0:T(8,128)S(1)}, f32[2560,1,128]{2,0,1:T(8,128)S(1)}, f32[2560,1,128]{2,0,1:T(8,128)}) %tuple.279, (s32[512]{0:T(512)}, s32[]{:T(128)}, ...), branch_computations={%region_17.16_spmd, %region_18.17_spmd} | conditional | flops 1353842688 | bytes 27500722 | solution.py:193
  227.4 2.9 fusion.67
  230.3 2.4 fusion.34
  238.7 9.8 %conditional.6 = ((f32[1,4,512,128]{3,2,1,0:T(8,128)S(1)}, f32[2560,1,128]{2,0,1:T(8,128)S(1)}, f32[2560,1,128]{2,0,1:T(8,128)})) conditional(s32[]{:T(128)} %bitcast.235, (f32[1,4,512,128]{3,2,1,0:T(8,128)S(1)}, f32[2560,1,128]{2,0,1:T(8,128)S(1)}, f32[2560,1,128]{2,0,1:T(8,128)}) %tuple.279, (s32[512]{0:T(512)}, s32[]{:T(128)}, ...), branch_computations={%region_17.16_spmd, %region_18.17_spmd} | conditional | flops 1353842688 | bytes 27500722 | solution.py:193
  241.6 2.9 fusion.67
  244.5 2.4 fusion.34
  252.9 9.8 %conditional.6 = ((f32[1,4,512,128]{3,2,1,0:T(8,128)S(1)}, f32[2560,1,128]{2,0,1:T(8,128)S(1)}, f32[2560,1,128]{2,0,1:T(8,128)})) conditional(s32[]{:T(128)} %bitcast.235, (f32[1,4,512,128]{3,2,1,0:T(8,128)S(1)}, f32[2560,1,128]{2,0,1:T(8,128)S(1)}, f32[2560,1,128]{2,0,1:T(8,128)}) %tuple.279, (s32[512]{0:T(512)}, s32[]{:T(128)}, ...), branch_computations={%region_17.16_spmd, %region_18.17_spmd} | conditional | flops 1353842688 | bytes 27500722 | solution.py:193
  255.8 2.9 fusion.67
  258.7 2.4 fusion.34
  282.9 41.4 %while.158 = (s32[]{:T(128)}, f32[1,4,512,128]{3,2,1,0:T(8,128)S(1)}, f32[2560,1,128]{2,0,1:T(8,128)S(1)}, f32[2560,1,128]{2,0,1:T(8,128)}, s32[2560]{0:T(1024)}...) while((s32[]{:T(128)}, ...), condition=%wide.region_19.19_spmd, body=%wide.region_16.18_spmd.sunk | while | flops 1353842688 | bytes 27501196 | solution.py:198
  300.3 9.8 %conditional.6 = ((f32[1,4,512,128]{3,2,1,0:T(8,128)S(1)}, f32[2560,1,128]{2,0,1:T(8,128)S(1)}, f32[2560,1,128]{2,0,1:T(8,128)})) conditional(s32[]{:T(128)} %bitcast.235, (f32[1,4,512,128]{3,2,1,0:T(8,128)S(1)}, f32[2560,1,128]{2,0,1:T(8,128)S(1)}, f32[2560,1,128]{2,0,1:T(8,128)}) %tuple.279, (s32[512]{0:T(512)}, s32[]{:T(128)}, ...), branch_computations={%region_17.16_spmd, %region_18.17_spmd} | conditional | flops 1353842688 | bytes 27500722 | solution.py:193
  303.2 2.9 fusion.67
  306.1 2.4 fusion.34
  314.5 9.8 %conditional.6 = ((f32[1,4,512,128]{3,2,1,0:T(8,128)S(1)}, f32[2560,1,128]{2,0,1:T(8,128)S(1)}, f32[2560,1,128]{2,0,1:T(8,128)})) conditional(s32[]{:T(128)} %bitcast.235, (f32[1,4,512,128]{3,2,1,0:T(8,128)S(1)}, f32[2560,1,128]{2,0,1:T(8,128)S(1)}, f32[2560,1,128]{2,0,1:T(8,128)}) %tuple.279, (s32[512]{0:T(512)}, s32[]{:T(128)}, ...), branch_computations={%region_17.16_spmd, %region_18.17_spmd} | conditional | flops 1353842688 | bytes 27500722 | solution.py:193
  317.3 2.9 fusion.67
  320.2 2.4 fusion.34
  327.4 1.9 collective-permute-start.6
  330.0 1.9 collective-permute-start.5
  331.9 5.1 %collective-permute-start.4 = (bf16[1024,128]{1,0:T(8,128)(2,1)S(1)}, bf16[1024,128]{1,0:T(8,128)(2,1)S(1)}, u32[]{:S(2)}, u32[]{:S(2)}) collective-permute-start(bf16[1024,128]{1,0:T(8,128)(2,1)S(1)} %slice_bitcast_fusion.1), channel_id=1, source_target_pairs={{8,0},{16,8},{24,16},{32,24},{40,32},{48,40},{56,48},{64,56},{72,6... | collective-permute-start | bytes 786440 | tf_op jit(solution)/shard_map/ppermute | solution.py:14
  337.7 1.9 collective-permute-start.7
  341.5 4.6 %all-to-all-start.3 = ((bf16[8,128,512]{2,1,0:T(8,128)(2,1)}), bf16[8,128,512]{2,1,0:T(8,128)(2,1)S(1)}, u32[]{:S(2)}, u32[]{:S(2)}) async-start(bf16[8,128,512]{2,1,0:T(8,128)(2,1)} %bitcast.241), calls=%async_computation.3 | async-start | bytes 2097152 | tf_op jit(solution)/shard_map/all_to_all | solution.py:233
  346.1 6.7 %collective-permute-done.7 = bf16[512,128]{1,0:T(8,128)(2,1)S(1)} collective-permute-done((bf16[512,128]{1,0:T(8,128)(2,1)}, bf16[512,128]{1,0:T(8,128)(2,1)S(1)}, u32[]{:S(2)}, u32[]{:S(2)}) %collective-permute-start.7) | collective-permute-done | bytes 131104 | tf_op jit(solution)/shard_map/ppermute | solution.py:14
  358.2 3.8 %all-to-all-done.3 = bf16[8,128,512]{2,1,0:T(8,128)(2,1)S(1)} async-done(((bf16[8,128,512]{2,1,0:T(8,128)(2,1)}), bf16[8,128,512]{2,1,0:T(8,128)(2,1)S(1)}, u32[]{:S(2)}, u32[]{:S(2)}) %all-to-all-start.3) | async-done | bytes 1048608 | tf_op jit(solution)/shard_map/all_to_all | solution.py:233
  (337 shorter events, 155.9 us)
Async XLA Ops:
  0.6 6.7 %copy-start.3 = (bf16[1024,128]{1,0:T(8,128)(2,1)S(1)}, bf16[1024,128]{1,0:T(8,128)(2,1)}, u32[]{:S(2)}) copy-start(bf16[1024,128]{1,0:T(8,128)(2,1)} %param.27) | copy-start | bytes 786436
  0.6 16.4 %copy-start.2 = (bf16[1024,128]{1,0:T(8,128)(2,1)S(1)}, bf16[1024,128]{1,0:T(8,128)(2,1)}, u32[]{:S(2)}) copy-start(bf16[1024,128]{1,0:T(8,128)(2,1)} %param.26) | copy-start | bytes 786436
  0.7 24.9 %copy-start.9 = (s32[32]{0:T(128)S(1)}, s32[32]{0:T(128)}, u32[]{:S(2)}) copy-start(s32[32]{0:T(128)} %param.29) | copy-start | bytes 388
  0.7 25.1 %copy-start.1 = (bf16[128,4096]{1,0:T(8,128)(2,1)S(1)}, bf16[128,4096]{1,0:T(8,128)(2,1)}, u32[]{:S(2)}) copy-start(bf16[128,4096]{1,0:T(8,128)(2,1)} %param.28) | copy-start | bytes 3145732
  3.0 24.1 %all-to-all-start = ((bf16[128,8,512]{0,2,1:T(8,128)(2,1)}), bf16[128,8,512]{0,2,1:T(8,128)(2,1)S(1)}, u32[]{:S(2)}, u32[]{:S(2)}) async-start(bf16[128,8,512]{0,2,1:T(8,128)(2,1)} %bitcast.44), calls=%async_computation | async-start | bytes 2097152 | tf_op jit(solution)/shard_map/all_to_all | solution.py:40
  7.4 32.1 %collective-permute-start.3 = (bf16[1024,128]{1,0:T(8,128)(2,1)S(1)}, bf16[1024,128]{1,0:T(8,128)(2,1)S(1)}, u32[]{:S(2)}, u32[]{:S(2)}) collective-permute-start(bf16[1024,128]{1,0:T(8,128)(2,1)S(1)} %copy-done.3), channel_id=1, source_target_pairs={{0,8},{8,16},{16,24},{24,32},{32,40},{40,48},{48,56},{56,64},{64,7... | collective-permute-start | bytes 786440 | tf_op jit(solution)/shard_map/ppermute | solution.py:14
  11.9 27.6 %collective-permute-start.2 = (bf16[512,128]{1,0:T(8,128)(2,1)}, bf16[512,128]{1,0:T(8,128)(2,1)}, u32[]{:S(2)}, u32[]{:S(2)}) collective-permute-start(bf16[512,128]{1,0:T(8,128)(2,1)} %slice.77), channel_id=1, source_target_pairs={{0,16},{8,24},{16,32},{24,40},{32,48},{40,56},{48,64},{56,72},{64,... | collective-permute-start | bytes 393224 | tf_op jit(solution)/shard_map/ppermute | solution.py:14
  17.0 21.4 %collective-permute-start.1 = (bf16[1024,128]{1,0:T(8,128)(2,1)S(1)}, bf16[1024,128]{1,0:T(8,128)(2,1)}, u32[]{:S(2)}, u32[]{:S(2)}) collective-permute-start(bf16[1024,128]{1,0:T(8,128)(2,1)S(1)} %copy-done.2), channel_id=1, source_target_pairs={{0,8},{8,16},{16,24},{24,32},{32,40},{40,48},{48,56},{56,64},{64,7... | collective-permute-start | bytes 786440 | tf_op jit(solution)/shard_map/ppermute | solution.py:14
  22.1 15.7 %collective-permute-start = (bf16[512,128]{1,0:T(8,128)(2,1)S(1)}, bf16[512,128]{1,0:T(8,128)(2,1)S(1)}, u32[]{:S(2)}, u32[]{:S(2)}) collective-permute-start(bf16[512,128]{1,0:T(8,128)(2,1)S(1)} %slice.76), channel_id=1, source_target_pairs={{0,16},{8,24},{16,32},{24,40},{32,48},{40,56},{48,64},{56,72},{64,... | collective-permute-start | bytes 393224 | tf_op jit(solution)/shard_map/ppermute | solution.py:14
  27.1 20.8 %all-to-all-start.2 = ((bf16[128,8,512]{0,2,1:T(8,128)(2,1)}), bf16[128,8,512]{0,2,1:T(8,128)(2,1)S(1)}, u32[]{:S(2)}, u32[]{:S(2)}) async-start(bf16[128,8,512]{0,2,1:T(8,128)(2,1)} %bitcast.51), calls=%async_computation.2 | async-start | bytes 2097152 | tf_op jit(solution)/shard_map/all_to_all | solution.py:139
  37.8 0.7 copy-start.8
  179.9 161.6 %all-to-all-start.1 = ((bf16[8,128,512]{2,1,0:T(8,128)(2,1)}), bf16[8,128,512]{2,1,0:T(8,128)(2,1)}, u32[]{:S(2)}, u32[]{:S(2)}) async-start(bf16[8,128,512]{2,1,0:T(8,128)(2,1)} %bitcast.48), calls=%async_computation.1 | async-start | bytes 2097152 | tf_op jit(solution)/shard_map/all_to_all | solution.py:138
  191.8 5.7 %copy-start.6 = (s32[1024]{0:T(1024)}, s32[1024]{0:T(1024)S(1)}, u32[]{:S(2)}) copy-start(s32[1024]{0:T(1024)S(1)} %get-tuple-element.3493) | copy-start | bytes 12292 | tf_op jit(solution)/shard_map/while
  212.2 1.0 copy-start
  212.3 1.0 copy-start.4
  213.3 2.9 copy-start.5
  226.4 1.0 copy-start
  226.4 1.0 copy-start.4
  227.4 2.9 copy-start.5
  240.5 1.0 copy-start
  240.6 1.0 copy-start.4
  241.6 2.9 copy-start.5
  254.7 1.0 copy-start
  254.7 1.0 copy-start.4
  255.8 2.9 copy-start.5
  267.1 1.6 copy-start.7
  268.7 5.7 %copy-start.6 = (s32[1024]{0:T(1024)}, s32[1024]{0:T(1024)S(1)}, u32[]{:S(2)}) copy-start(s32[1024]{0:T(1024)S(1)} %get-tuple-element.3493) | copy-start | bytes 12292 | tf_op jit(solution)/shard_map/while
  302.1 1.0 copy-start
  302.1 1.0 copy-start.4
  303.2 2.9 copy-start.5
  316.3 1.0 copy-start
  316.3 1.0 copy-start.4
  317.3 2.9 copy-start.5
  324.3 1.6 copy-start.7
  327.4 13.0 %collective-permute-start.6 = (bf16[1024,128]{1,0:T(8,128)(2,1)S(1)}, bf16[1024,128]{1,0:T(8,128)(2,1)S(1)}, u32[]{:S(2)}, u32[]{:S(2)}) collective-permute-start(bf16[1024,128]{1,0:T(8,128)(2,1)S(1)} %slice_bitcast_fusion), channel_id=1, source_target_pairs={{8,0},{16,8},{24,16},{32,24},{40,32},{48,40},{56,48},{64,56},{72,6... | collective-permute-start | bytes 786440 | tf_op jit(solution)/shard_map/ppermute | solution.py:14
  330.0 23.6 %collective-permute-start.5 = (bf16[512,128]{1,0:T(8,128)(2,1)}, bf16[512,128]{1,0:T(8,128)(2,1)}, u32[]{:S(2)}, u32[]{:S(2)}) collective-permute-start(bf16[512,128]{1,0:T(8,128)(2,1)} %slice_bitcast_fusion.3), channel_id=1, source_target_pairs={{16,0},{24,8},{32,16},{40,24},{48,32},{56,40},{64,48},{72,56},{80,... | collective-permute-start | bytes 393224 | tf_op jit(solution)/shard_map/ppermute | solution.py:14
  331.9 21.6 %collective-permute-start.4 = (bf16[1024,128]{1,0:T(8,128)(2,1)S(1)}, bf16[1024,128]{1,0:T(8,128)(2,1)S(1)}, u32[]{:S(2)}, u32[]{:S(2)}) collective-permute-start(bf16[1024,128]{1,0:T(8,128)(2,1)S(1)} %slice_bitcast_fusion.1), channel_id=1, source_target_pairs={{8,0},{16,8},{24,16},{32,24},{40,32},{48,40},{56,48},{64,56},{72,6... | collective-permute-start | bytes 786440 | tf_op jit(solution)/shard_map/ppermute | solution.py:14
  337.7 15.1 %collective-permute-start.7 = (bf16[512,128]{1,0:T(8,128)(2,1)}, bf16[512,128]{1,0:T(8,128)(2,1)S(1)}, u32[]{:S(2)}, u32[]{:S(2)}) collective-permute-start(bf16[512,128]{1,0:T(8,128)(2,1)} %slice_bitcast_fusion.2), channel_id=1, source_target_pairs={{16,0},{24,8},{32,16},{40,24},{48,32},{56,40},{64,48},{72,56},{80,... | collective-permute-start | bytes 393224 | tf_op jit(solution)/shard_map/ppermute | solution.py:14
  341.5 20.5 %all-to-all-start.3 = ((bf16[8,128,512]{2,1,0:T(8,128)(2,1)}), bf16[8,128,512]{2,1,0:T(8,128)(2,1)S(1)}, u32[]{:S(2)}, u32[]{:S(2)}) async-start(bf16[8,128,512]{2,1,0:T(8,128)(2,1)} %bitcast.241), calls=%async_computation.3 | async-start | bytes 2097152 | tf_op jit(solution)/shard_map/all_to_all | solution.py:233
where the time goes:
time: 368 us; the launch traced here: 364 us
  local copies, waits for them, and re-layouts  116 us (32%)
  loops' own time  85.7 us (23%)
  matrix products  67.9 us (18%)
  starting transfers between devices  46.3 us (13%)
  other arithmetic  28.8 us (8%)
  waiting for transfers between devices  18.7 us (5%)
    dynamic_slice x34, local copies, waits for them, and re-layouts, needed(): reaches = win_pos[col_start] <= own_pos[row_start + block_rows - 1]  28.3 us
    ppermute x8, starting transfers between devices, from_behind(): return lax.ppermute(value, axis, pairs)  28.2 us
    another operation x2, loops' own time, forward_block(): lax.fori_loop(0, k_blocks, stats_step, (jnp.full(stat_shape, -1e+30, jnp....  27.1 us
    another operation x2, loops' own time, forward_block(): lax.fori_loop(0, k_blocks, value_step, jnp.zeros((kv_local, group_size, b...  26 us
    another operation x2, loops' own time, backward_block(): lax.fori_loop(0, k_blocks, grad_step, (q_start, key_acc, value_acc))  24.7 us
    dynamic_slice x34, local copies, waits for them, and re-layouts, needed(): return reaches & (win_doc[col_start + block_rows - 1] >= own_doc[row_start])  24.2 us
    dot_general x6, matrix products, grad_compute(): jnp.einsum('gjqk,qgjd->kgd', weights, g_tile, preferred_element_type=jnp....  17.4 us
    dot_general x6, matrix products, value_compute(): jnp.einsum('gjqk,kgd->gjqd', weights, v_tile, preferred_element_type=jnp....  16.8 us
  transfers between devices with their start and end apart: 12, of which 5 were waited for; matrix products, arithmetic and copies ran while one was open for 35% of the time, Pallas kernels for 0%

commit v1 on v0

v1 whole, which is shorter than its diff:
```python
import functools
import math

import jax
import jax.numpy as jnp
from jax import lax
from jax.experimental import pallas as pl
from jax.experimental.pallas import tpu as pltpu
from jax.sharding import PartitionSpec as P

HEAD = 128
QH = 32
KVH = 8
TILE = 128
SHARD = 1024
REACH = 11
WIN = REACH + 1
GROUP = QH // KVH
COLS = GROUP * HEAD
TILES = SHARD // TILE
NEAR = SHARD
FAR = REACH * TILE - SHARD
BACK = NEAR + FAR
ROWS = BACK + SHARD
CHUNK = 256
FACTOR = HEAD**-0.5
SCALE = FACTOR * math.log2(math.e)
LOW = -1e30
F32 = jnp.float32
BF16 = jnp.bfloat16
MESH = pl.DeviceIdType.MESH


def mm(a, b):
    return jnp.dot(a, b, preferred_element_type=F32)


def fold(x, op):
    return op(x.reshape(x.shape[0] // 8, 8, x.shape[1]), axis=0)


def flip(x):
    return jnp.concatenate([x[:, h * HEAD : (h + 1) * HEAD].T for h in range(GROUP)], axis=1)


def stack(x):
    return jnp.concatenate([x[:, h * HEAD : (h + 1) * HEAD] for h in range(GROUP)], axis=0)


def attend(base, bias, q, g, k_win, v_win, k_flip, v_flip, k_sum, v_sum, s_buf, p_buf, d_buf):
    q_flip, q_rows = flip(q), stack(q)
    count = WIN * TILE // CHUNK
    per = CHUNK // TILE
    top = jnp.full((8, COLS), LOW, F32)
    for c in range(count):
        s = mm(k_win[pl.ds(base + c * CHUNK, CHUNK), :], q_flip)
        if c == count - 1:
            key = lax.broadcasted_iota(jnp.int32, (TILE, COLS), 0)
            tok = lax.broadcasted_iota(jnp.int32, (TILE, COLS), 1) % TILE
            last = jnp.where(key <= tok, s[CHUNK - TILE :], LOW)
            s = jnp.concatenate([s[: CHUNK - TILE], last], axis=0)
        s_buf[c * CHUNK : (c + 1) * CHUNK, :] = s
        for u in range(per):
            top = jnp.maximum(top, fold(s[u * TILE : (u + 1) * TILE], jnp.max) + bias[c * per + u])
    top = jnp.max(top, axis=0, keepdims=True)
    total = jnp.zeros((8, COLS), F32)
    for c in range(WIN):
        rows = slice(c * TILE, (c + 1) * TILE)
        p = jnp.exp2((s_buf[rows, :] - (top - bias[c])) * SCALE)
        total = total + fold(p, jnp.sum)
        p_buf[rows, :] = p.astype(BF16)
    inverse = 1.0 / jnp.sum(total, axis=0, keepdims=True)
    out = (mm(v_flip[:, pl.ds(base, WIN * TILE)], p_buf[...]) * inverse).astype(BF16)
    g_flip = (flip(g).astype(F32) * inverse).astype(BF16)
    g_rows = stack(flip(g_flip))
    delta = jnp.sum(g_flip.astype(F32) * out.astype(F32), axis=0, keepdims=True)
    for c in range(count):
        rows = slice(c * CHUNK, (c + 1) * CHUNK)
        keys = pl.ds(base + c * CHUNK, CHUNK)
        p = p_buf[rows, :]
        d_prob = mm(v_win[keys, :], g_flip)
        d_score = (p.astype(F32) * (d_prob - delta)).astype(BF16)
        d_buf[rows, :] = d_score
        v_sum[keys, :] += mm(p, g_rows)
        k_sum[keys, :] += mm(d_score, q_rows)
    d_query = (mm(k_flip[:, pl.ds(base, WIN * TILE)], d_buf[...]) * FACTOR).astype(BF16)
    return flip(out), flip(d_query)


def kernel(
    seqs, starts, q_in, k_in, v_in, g_in, o_out, dq_out, dk_out, dv_out,
    q_buf, g_buf, o_buf, dq_buf, k_win, v_win, k_flip, v_flip, k_sum, v_sum, s_buf, p_buf, d_buf,
    k_part, v_part, k_near, v_near, k_far, v_far,
    in_send, q_recv, g_recv, out_send, o_recv, dq_recv, z_send, z_recv,
):
    s, h = lax.axis_index("seq"), lax.axis_index("head")
    x, core = h // 2, h % 2

    def head_of(dx, dc):
        return ((x + dx) % 4) * 2 + (core + dc) % 2

    def seq_of(by):
        return (s + by + seqs) % seqs

    barrier = pltpu.get_barrier_semaphore()
    others = [(s, head_of(dx, dc)) for dx in range(4) for dc in range(2) if dx or dc]
    others += [(seq_of(by), h) for by in (1, 2, -1, -2)]
    for other in others:
        pl.semaphore_signal(barrier, inc=1, device_id=other, device_id_type=MESH)
    pl.semaphore_wait(barrier, len(others))

    def cols(head):
        return pl.ds(pl.multiple_of(head * COLS, COLS), COLS)

    def send(src, dst, send_sem, recv_sem, to):
        copy = pltpu.make_async_remote_copy(
            src_ref=src, dst_ref=dst, send_sem=send_sem, recv_sem=recv_sem, device_id=to, device_id_type=MESH
        )
        copy.start()
        return copy

    kv = []
    for n, (src, dst) in enumerate(((k_in, k_win), (v_in, v_win))):
        kv.append(send(src, dst.at[pl.ds(FAR, NEAR)], z_send.at[n], z_recv.at[n], (seq_of(1), h)))
    for n, (src, dst) in enumerate(((k_in, k_win), (v_in, v_win))):
        kv.append(
            send(src.at[pl.ds(SHARD - FAR, FAR)], dst.at[pl.ds(0, FAR)], z_send.at[2 + n], z_recv.at[2 + n], (seq_of(2), h))
        )
    own = [
        pltpu.make_async_copy(k_in, k_win.at[pl.ds(BACK, SHARD)], z_recv.at[4]),
        pltpu.make_async_copy(v_in, v_win.at[pl.ds(BACK, SHARD)], z_recv.at[5]),
        pltpu.make_async_copy(q_in.at[:, cols(h)], q_buf.at[h], q_recv.at[h]),
        pltpu.make_async_copy(g_in.at[:, cols(h)], g_buf.at[h], g_recv.at[h]),
    ]
    for copy in own:
        copy.start()
    ins = []
    for n in range(1, 8):
        to = head_of(-(n // 2) + 4, n % 2)
        ins.append(send(q_in.at[:, cols(to)], q_buf.at[h], in_send.at[2 * n], q_recv.at[h], (s, to)))
        ins.append(send(g_in.at[:, cols(to)], g_buf.at[h], in_send.at[2 * n + 1], g_recv.at[h], (s, to)))

    k_sum[...] = jnp.zeros_like(k_sum)
    v_sum[...] = jnp.zeros_like(v_sum)
    own[0].wait()
    own[1].wait()
    for copy in kv:
        copy.wait_recv()

    def turn(j, carry):
        at = pl.ds(pl.multiple_of(j * TILE, TILE), TILE)
        k_flip[:, at] = k_win[at, :].T
        v_flip[:, at] = v_win[at, :].T
        return carry

    lax.fori_loop(0, ROWS // TILE, turn, 0)

    def arrived(buf, i, sem):
        pltpu.make_async_copy(buf.at[i], buf.at[i], sem.at[i]).wait()

    def step(r, carry):
        i = head_of(r // 2, r % 2)
        tile = s * TILES + i
        begin = jnp.int32(0)
        for n in range(starts.shape[0]):
            begin = jnp.maximum(begin, jnp.where(starts[n] <= tile * TILE, starts[n], 0))
        bias = [jnp.where((tile - REACH + c) * TILE >= begin, 0.0, LOW).astype(F32) for c in range(WIN)]
        arrived(q_buf, i, q_recv)
        arrived(g_buf, i, g_recv)
        out, d_query = attend(
            pl.multiple_of(i * TILE, TILE), bias, q_buf[i], g_buf[i], k_win, v_win, k_flip, v_flip, k_sum, v_sum,
            s_buf, p_buf, d_buf,
        )
        o_buf[i] = out
        dq_buf[i] = d_query

        @pl.when(r == 0)
        def _():
            pltpu.make_async_copy(o_buf.at[i], o_out.at[:, cols(h)], o_recv.at[h]).start()
            pltpu.make_async_copy(dq_buf.at[i], dq_out.at[:, cols(h)], dq_recv.at[h]).start()

        @pl.when(r > 0)
        def _():
            send(o_buf.at[i], o_out.at[:, cols(h)], out_send.at[2 * r], o_recv.at[h], (s, i))
            send(dq_buf.at[i], dq_out.at[:, cols(h)], out_send.at[2 * r + 1], dq_recv.at[h], (s, i))

        return carry

    lax.fori_loop(0, 8, step, 0)

    def part(j, carry):
        at = pl.ds(pl.multiple_of(j * TILE, TILE), TILE)
        k_part[at, :] = k_sum[at, :].astype(BF16)
        v_part[at, :] = v_sum[at, :].astype(BF16)
        return carry

    lax.fori_loop(0, BACK // TILE, part, 0)
    parts = []
    for n, (src, near, far) in enumerate(((k_part, k_near, k_far), (v_part, v_near, v_far))):
        parts.append(send(src.at[pl.ds(0, FAR)], far, z_send.at[4 + n], z_recv.at[6 + n], (seq_of(-2), h)))
        parts.append(send(src.at[pl.ds(FAR, NEAR)], near, z_send.at[6 + n], z_recv.at[8 + n], (seq_of(-1), h)))
    for copy in parts:
        copy.wait_recv()

    def total(j, carry):
        at = pl.ds(pl.multiple_of(j * TILE, TILE), TILE)
        full = pl.ds(pl.multiple_of(BACK + j * TILE, TILE), TILE)
        k_sum[full, :] += k_near[at, :].astype(F32)
        v_sum[full, :] += v_near[at, :].astype(F32)
        return carry

    lax.fori_loop(0, TILES, total, 0)

    def total_far(j, carry):
        at = pl.ds(pl.multiple_of(j * TILE, TILE), TILE)
        full = pl.ds(pl.multiple_of(ROWS - FAR + j * TILE, TILE), TILE)
        k_sum[full, :] += k_far[at, :].astype(F32)
        v_sum[full, :] += v_far[at, :].astype(F32)
        return carry

    lax.fori_loop(0, FAR // TILE, total_far, 0)
    dk_out[...] = (k_sum[pl.ds(BACK, SHARD), :] * FACTOR).astype(BF16)
    dv_out[...] = v_sum[pl.ds(BACK, SHARD), :].astype(BF16)

    for copy in kv + ins + parts:
        copy.wait_send()

    def finish(i, carry):
        pltpu.make_async_copy(o_buf.at[i], o_buf.at[i], o_recv.at[i]).wait()
        pltpu.make_async_copy(dq_buf.at[i], dq_buf.at[i], dq_recv.at[i]).wait()
        return carry

    lax.fori_loop(0, 8, finish, 0)

    def sent(n, carry):
        pltpu.make_async_copy(o_buf.at[0], o_buf.at[0], out_send.at[n]).wait()
        return carry

    lax.fori_loop(2, 16, sent, 0)


def local(seqs, queries, key_heads, value_heads, output_grad, doc_starts):
    vmem = pl.BlockSpec(memory_space=pltpu.VMEM)
    hbm = pl.BlockSpec(memory_space=pl.ANY)
    dma = pltpu.SemaphoreType.DMA
    return pl.pallas_call(
        functools.partial(kernel, seqs),
        out_shape=[
            jax.ShapeDtypeStruct(queries.shape, BF16),
            jax.ShapeDtypeStruct(queries.shape, BF16),
            jax.ShapeDtypeStruct(key_heads.shape, BF16),
            jax.ShapeDtypeStruct(key_heads.shape, BF16),
        ],
        in_specs=[pl.BlockSpec(memory_space=pltpu.SMEM), hbm, hbm, hbm, hbm],
        out_specs=[hbm, hbm, vmem, vmem],
        scratch_shapes=[pltpu.VMEM((TILES, TILE, COLS), BF16)] * 4
        + [pltpu.VMEM((ROWS, HEAD), BF16)] * 2
        + [pltpu.VMEM((HEAD, ROWS), BF16)] * 2
        + [pltpu.VMEM((ROWS, HEAD), F32)] * 2
        + [pltpu.VMEM((WIN * TILE, COLS), F32)]
        + [pltpu.VMEM((WIN * TILE, COLS), BF16)] * 2
        + [pltpu.VMEM((BACK, HEAD), BF16)] * 2
        + [pltpu.VMEM((NEAR, HEAD), BF16)] * 2
        + [pltpu.VMEM((FAR, HEAD), BF16)] * 2
        + [dma((16,)), dma((8,)), dma((8,)), dma((16,)), dma((8,)), dma((8,)), dma((8,)), dma((10,))],
        compiler_params=pltpu.CompilerParams(
            collective_id=0, has_side_effects=True, vmem_limit_bytes=48 << 20
        ),
        cost_estimate=pl.CostEstimate(flops=10**10, bytes_accessed=8 << 20, transcendentals=6 << 20),
        name="attention",
    )(doc_starts, queries, key_heads, value_heads, output_grad)


def solution(mesh):
    wide = P(("seq", "head"), None)
    narrow = P("seq", "head")
    return jax.shard_map(
        functools.partial(local, mesh.shape["seq"]),
        mesh=mesh,
        in_specs=(wide, narrow, narrow, wide, P()),
        out_specs=(wide, wide, narrow, narrow),
        check_vma=False,
    )
```

time: 368 us -> 89.4 us (0.24)
  the two profiles are of different devices: /device:TPU:8 before, /device:TPU:1 now
where the time goes in v1:
time: 89.4 us; the launch traced here: 89.2 us
  Pallas kernels  80.2 us (90%)
  local copies, waits for them, and re-layouts  8.34 us (9%)
    pallas_call x1, Pallas kernels, local(): pl.pallas_call(functools.partial(kernel, seqs), out_shape=[jax.ShapeDtype...  80.2 us
    unnamed x14, local copies, waits for them, and re-layouts  8.34 us

profile of v1, /device:TPU:1, one launch (start us, length us, event | category | flops | bytes accessed | tf_op | source)
XLA Modules:
  0.0 89.2 jit_solution(17091975732388269342)
XLA Ops:
  0.6 0.0 copy-start
  0.6 1.2 %copy-done = bf16[128,4096]{1,0:T(8,128)(2,1)S(1)} copy-done((bf16[128,4096]{1,0:T(8,128)(2,1)S(1)}, bf16[128,4096]{1,0:T(8,128)(2,1)}, u32[]{:S(2)}) %copy-start) | copy-done | bytes 1048600
  1.9 0.0 copy-start.1
  1.9 1.2 %copy-done.1 = bf16[128,4096]{1,0:T(8,128)(2,1)S(1)} copy-done((bf16[128,4096]{1,0:T(8,128)(2,1)S(1)}, bf16[128,4096]{1,0:T(8,128)(2,1)}, u32[]{:S(2)}) %copy-start.1) | copy-done | bytes 1048600
  3.1 0.0 copy-start.2
  3.1 0.9 %copy-done.2 = bf16[1024,128]{1,0:T(8,128)(2,1)S(1)} copy-done((bf16[1024,128]{1,0:T(8,128)(2,1)S(1)}, bf16[1024,128]{1,0:T(8,128)(2,1)}, u32[]{:S(2)}) %copy-start.2) | copy-done | bytes 262168
  4.0 0.0 copy-start.3
  4.0 0.9 %copy-done.3 = bf16[1024,128]{1,0:T(8,128)(2,1)S(1)} copy-done((bf16[1024,128]{1,0:T(8,128)(2,1)S(1)}, bf16[1024,128]{1,0:T(8,128)(2,1)}, u32[]{:S(2)}) %copy-start.3) | copy-done | bytes 262168
  5.0 0.0 copy-start.4
  5.0 0.7 copy-done.4
  5.6 80.2 %attention.1 = (bf16[128,4096]{1,0:T(8,128)(2,1)S(1)}, bf16[128,4096]{1,0:T(8,128)(2,1)S(1)}, bf16[1024,128]{1,0:T(8,128)(2,1)S(1)}, bf16[1024,128]{1,0:T(8,128)(2,1)S(1)}) custom-call(s32[32]{0:T(128)S(1)} %copy-done.4, bf16[128,4096]{1,0:T(8,128)(2,1)S(1)} %copy-done, bf16[1024,128]{1,0:T(8,128)(2,1)S(1)} %copy-done.2, bf16[1024,128]{1,0:T(8,128)(2,1)S(1)} %copy-done.3, ...), custom_call_target="tpu_custom_call" | custom-call | flops 10000000000 | bytes 8388608 | tf_op jit(solution)/shard_map/attention/pallas_call | solution.py:246
  85.8 1.0 %copy.13 = bf16[128,4096]{1,0:T(8,128)(2,1)} copy(bf16[128,4096]{1,0:T(8,128)(2,1)S(1)} %get-tuple-element.8) | data formatting | bytes 2097152
  86.8 1.0 %copy.14 = bf16[128,4096]{1,0:T(8,128)(2,1)} copy(bf16[128,4096]{1,0:T(8,128)(2,1)S(1)} %get-tuple-element.9) | data formatting | bytes 2097152
  87.8 0.7 copy.15
  88.5 0.7 copy.16
Async XLA Ops:
  0.6 1.2 %copy-start = (bf16[128,4096]{1,0:T(8,128)(2,1)S(1)}, bf16[128,4096]{1,0:T(8,128)(2,1)}, u32[]{:S(2)}) copy-start(bf16[128,4096]{1,0:T(8,128)(2,1)} %q_in.1) | copy-start | bytes 3145732
  1.9 1.2 %copy-start.1 = (bf16[128,4096]{1,0:T(8,128)(2,1)S(1)}, bf16[128,4096]{1,0:T(8,128)(2,1)}, u32[]{:S(2)}) copy-start(bf16[128,4096]{1,0:T(8,128)(2,1)} %g_in.1) | copy-start | bytes 3145732
  3.1 0.9 %copy-start.2 = (bf16[1024,128]{1,0:T(8,128)(2,1)S(1)}, bf16[1024,128]{1,0:T(8,128)(2,1)}, u32[]{:S(2)}) copy-start(bf16[1024,128]{1,0:T(8,128)(2,1)} %k_in.1) | copy-start | bytes 786436
  4.0 0.9 %copy-start.3 = (bf16[1024,128]{1,0:T(8,128)(2,1)S(1)}, bf16[1024,128]{1,0:T(8,128)(2,1)}, u32[]{:S(2)}) copy-start(bf16[1024,128]{1,0:T(8,128)(2,1)} %v_in.1) | copy-start | bytes 786436
  5.0 0.7 copy-start.4

commit v2 on v1

v2 whole, which is shorter than its diff:
```python
import functools
import math

import jax
import jax.numpy as jnp
from jax import lax
from jax.experimental import pallas as pl
from jax.experimental.pallas import tpu as pltpu
from jax.sharding import PartitionSpec as P

HEAD = 128
QH = 32
KVH = 8
TILE = 128
SHARD = 1024
REACH = 11
WIN = REACH + 1
GROUP = QH // KVH
COLS = GROUP * HEAD
TILES = SHARD // TILE
NEAR = SHARD
FAR = REACH * TILE - SHARD
BACK = NEAR + FAR
ROWS = BACK + SHARD
CHUNK = 256
FACTOR = HEAD**-0.5
SCALE = FACTOR * math.log2(math.e)
LOW = -1e30
F32 = jnp.float32
BF16 = jnp.bfloat16
MESH = pl.DeviceIdType.MESH


def mm(a, b):
    return jnp.dot(a, b, preferred_element_type=F32)


def fold(x, op):
    return op(x.reshape(x.shape[0] // 8, 8, x.shape[1]), axis=0)


def flip(x):
    return jnp.concatenate([x[:, h * HEAD : (h + 1) * HEAD].T for h in range(GROUP)], axis=1)


def stack(x):
    return jnp.concatenate([x[:, h * HEAD : (h + 1) * HEAD] for h in range(GROUP)], axis=0)


def attend(base, bias, q, g, k_win, v_win, k_flip, v_flip, k_sum, v_sum, s_buf, p_buf, d_buf):
    q_flip, q_rows = flip(q), stack(q)
    count = WIN * TILE // CHUNK
    per = CHUNK // TILE
    top = jnp.full((8, COLS), LOW, F32)
    for c in range(count):
        s = mm(k_win[pl.ds(base + c * CHUNK, CHUNK), :], q_flip)
        if c == count - 1:
            key = lax.broadcasted_iota(jnp.int32, (TILE, COLS), 0)
            tok = lax.broadcasted_iota(jnp.int32, (TILE, COLS), 1) % TILE
            last = jnp.where(key <= tok, s[CHUNK - TILE :], LOW)
            s = jnp.concatenate([s[: CHUNK - TILE], last], axis=0)
        s_buf[c * CHUNK : (c + 1) * CHUNK, :] = s
        for u in range(per):
            top = jnp.maximum(top, fold(s[u * TILE : (u + 1) * TILE], jnp.max) + bias[c * per + u])
    top = jnp.max(top, axis=0, keepdims=True)
    total = jnp.zeros((8, COLS), F32)
    for c in range(WIN):
        rows = slice(c * TILE, (c + 1) * TILE)
        p = jnp.exp2((s_buf[rows, :] - (top - bias[c])) * SCALE)
        total = total + fold(p, jnp.sum)
        p_buf[rows, :] = p.astype(BF16)
    inverse = 1.0 / jnp.sum(total, axis=0, keepdims=True)
    out = (mm(v_flip[:, pl.ds(base, WIN * TILE)], p_buf[...]) * inverse).astype(BF16)
    g_flip = (flip(g).astype(F32) * inverse).astype(BF16)
    g_rows = stack(flip(g_flip))
    delta = jnp.sum(g_flip.astype(F32) * out.astype(F32), axis=0, keepdims=True)
    for c in range(count):
        rows = slice(c * CHUNK, (c + 1) * CHUNK)
        keys = pl.ds(base + c * CHUNK, CHUNK)
        p = p_buf[rows, :]
        d_prob = mm(v_win[keys, :], g_flip)
        d_score = (p.astype(F32) * (d_prob - delta)).astype(BF16)
        d_buf[rows, :] = d_score
        v_sum[keys, :] += mm(p, g_rows)
        k_sum[keys, :] += mm(d_score, q_rows)
    d_query = (mm(k_flip[:, pl.ds(base, WIN * TILE)], d_buf[...]) * FACTOR).astype(BF16)
    return flip(out), flip(d_query)


ORDER = (
    (6, 3, 0, 1, 2, 7, 4, 5),
    (7, 3, 0, 1, 2, 6, 4, 5),
    (4, 3, 2, 0, 1, 5, 6, 7),
    (5, 3, 2, 1, 0, 4, 6, 7),
    (6, 4, 5, 2, 3, 0, 1, 7),
    (7, 5, 4, 3, 2, 0, 1, 6),
    (6, 7, 4, 0, 1, 2, 3, 5),
    (7, 6, 5, 1, 0, 2, 3, 4),
)
PIECES = ((SHARD - 3 * TILE, 3 * TILE), (SHARD - 5 * TILE, 2 * TILE), (0, 3 * TILE))
CODE = [sum(tile * 8**n for n, tile in enumerate(row)) for row in ORDER]
FIRST_MID = [min(n for n, t in enumerate(row) if t < 6) for row in ORDER]
FIRST_FAR = [min(n for n, t in enumerate(row) if t < 3) for row in ORDER]
LAST_FAR = [max(n for n, t in enumerate(row) if t < 3) for row in ORDER]
LAST_MID = [max(n for n, t in enumerate(row) if t < 6) for row in ORDER]


def by_head(h, values):
    result = jnp.int32(values[0])
    for n in range(1, 8):
        result = jnp.where(h == n, values[n], result)
    return result


def kernel(
    seqs, starts_in, q_in, k_in, v_in, g_in, o_out, dq_out, dk_out, dv_out,
    starts, q_buf, g_buf, o_buf, dq_buf, k_win, v_win, k_flip, v_flip, k_sum, v_sum, s_buf, p_buf, d_buf,
    k_part, v_part, k_near, v_near, k_far, v_far,
    in_send, q_recv, g_recv, out_send, o_recv, dq_recv, z_send, z_recv,
):
    s, h = lax.axis_index("seq"), lax.axis_index("head")
    x, core = h // 2, h % 2
    has_next, has_prev = s < seqs - 1, s > 0
    after, before = (lax.rem(s + 1, seqs), h), (lax.rem(s + seqs - 1, seqs), h)

    def head_of(dx, dc):
        return ((x + dx) % 4) * 2 + (core + dc) % 2

    own = [
        pltpu.make_async_copy(starts_in, starts, z_recv.at[18]),
        pltpu.make_async_copy(k_in, k_win.at[pl.ds(BACK, SHARD)], z_recv.at[16]),
        pltpu.make_async_copy(v_in, v_win.at[pl.ds(BACK, SHARD)], z_recv.at[17]),
    ]
    for copy in own:
        copy.start()
    barrier = pltpu.get_barrier_semaphore()
    others = [(s, head_of(dx, dc)) for dx in range(4) for dc in range(2) if dx or dc]
    for other in others:
        pl.semaphore_signal(barrier, inc=1, device_id=other, device_id_type=MESH)

    @pl.when(has_next)
    def _():
        pl.semaphore_signal(barrier, inc=1, device_id=after, device_id_type=MESH)

    @pl.when(has_prev)
    def _():
        pl.semaphore_signal(barrier, inc=1, device_id=before, device_id_type=MESH)

    pl.semaphore_wait(barrier, len(others) + jnp.where(has_next, 1, 0) + jnp.where(has_prev, 1, 0))

    def cols(head):
        return pl.ds(pl.multiple_of(head * COLS, COLS), COLS)

    def remote(src, dst, send_sem, recv_sem, to):
        return pltpu.make_async_remote_copy(
            src_ref=src, dst_ref=dst, send_sem=send_sem, recv_sem=recv_sem, device_id=to, device_id_type=MESH
        )

    def start(copies):
        for copy in copies:
            copy.start()

    def took(copies):
        for copy in copies:
            copy.wait_recv()

    def gone(copies):
        for copy in copies:
            copy.wait_send()

    def regroup(n, dx, dc):
        to = head_of(dx, dc)
        copies = [
            remote(q_in.at[:, cols(to)], q_buf.at[h], in_send.at[2 * n], q_recv.at[h], (s, to)),
            remote(g_in.at[:, cols(to)], g_buf.at[h], in_send.at[2 * n + 1], g_recv.at[h], (s, to)),
        ]
        start(copies)
        return copies

    def shift(n, first, size):
        return [
            remote(src.at[pl.ds(first, size)], dst.at[pl.ds(FAR + first, size)], z_send.at[n + m], z_recv.at[n + m], after)
            for m, (src, dst) in enumerate(((k_in, k_win), (v_in, v_win)))
        ]

    near_in = [shift(2 * n, *piece) for n, piece in enumerate(PIECES)]
    far_in = [
        remote(win.at[pl.ds(BACK - FAR, FAR)], win.at[pl.ds(0, FAR)], z_send.at[6 + m], z_recv.at[6 + m], after)
        for m, win in enumerate((k_win, v_win))
    ]

    @pl.when(has_next)
    def _():
        start(near_in[0])

    first_ins = regroup(0, 1, 0) + regroup(1, 3, 0)

    @pl.when(has_next)
    def _():
        start(near_in[1])
        start(near_in[2])

    ins = regroup(2, 0, 1) + regroup(3, 1, 1) + regroup(4, 3, 1)
    start(
        [
            pltpu.make_async_copy(q_in.at[:, cols(h)], q_buf.at[h], q_recv.at[h]),
            pltpu.make_async_copy(g_in.at[:, cols(h)], g_buf.at[h], g_recv.at[h]),
        ]
    )

    def rows(j):
        return pl.ds(pl.multiple_of(j * TILE, TILE), TILE)

    def turn(j, carry):
        k_flip[:, rows(j)] = k_win[rows(j), :].T
        v_flip[:, rows(j)] = v_win[rows(j), :].T
        return carry

    def turn_piece(first, size):
        lax.fori_loop((FAR + first) // TILE, (FAR + first + size) // TILE, turn, 0)

    k_sum[...] = jnp.zeros_like(k_sum)
    v_sum[...] = jnp.zeros_like(v_sum)

    @pl.when(jnp.logical_not(has_prev))
    def _():
        for win in (k_win, v_win):
            win[0:BACK, :] = jnp.zeros((BACK, HEAD), BF16)

    @pl.when(jnp.logical_not(has_next))
    def _():
        for buf in (k_near, v_near, k_far, v_far):
            buf[...] = jnp.zeros_like(buf)

    for copy in own:
        copy.wait()
    lax.fori_loop(BACK // TILE, ROWS // TILE, turn, 0)

    @pl.when(has_prev)
    def _():
        took(near_in[0])

    @pl.when(has_next)
    def _():
        start(far_in)

    turn_piece(*PIECES[0])
    gone(first_ins)
    ins += regroup(5, 2, 0) + regroup(6, 2, 1)

    @pl.when(has_prev)
    def _():
        took(near_in[1])

    turn_piece(*PIECES[1])

    def arrived(buf, i, sem):
        pltpu.make_async_copy(buf.at[i], buf.at[i], sem.at[i]).wait()

    code = by_head(h, CODE)
    first_mid, first_far = by_head(h, FIRST_MID), by_head(h, FIRST_FAR)
    last_mid, last_far = by_head(h, LAST_MID), by_head(h, LAST_FAR)

    def to_part(j, carry):
        k_part[rows(j), :] = k_sum[rows(j), :].astype(BF16)
        v_part[rows(j), :] = v_sum[rows(j), :].astype(BF16)
        return carry

    parts = ((k_part, k_near, k_far), (v_part, v_near, v_far))
    far_back = [
        remote(part.at[pl.ds(0, FAR)], far, z_send.at[8 + m], z_recv.at[8 + m], before)
        for m, (part, near, far) in enumerate(parts)
    ]
    near_back = [
        [
            remote(
                part.at[pl.ds(FAR + first, size)], near.at[pl.ds(first, size)], z_send.at[10 + 2 * n + m],
                z_recv.at[10 + 2 * n + m] if n < 2 else z_recv.at[17 + 2 + m], before,
            )
            for m, (part, near, far) in enumerate(parts)
        ]
        for n, (first, size) in enumerate(PIECES[::-1])
    ]

    def step(r, left):
        i = left % 8
        tile = s * TILES + i
        begin = jnp.int32(0)
        for n in range(starts.shape[0]):
            begin = jnp.maximum(begin, jnp.where(starts[n] <= tile * TILE, starts[n], 0))
        bias = [jnp.where((tile - REACH + c) * TILE >= begin, 0.0, LOW).astype(F32) for c in range(WIN)]

        @pl.when(r == first_mid)
        def _():
            @pl.when(has_prev)
            def _():
                took(near_in[2])

            turn_piece(*PIECES[2])

        @pl.when(r == first_far)
        def _():
            @pl.when(has_prev)
            def _():
                took(far_in)

            lax.fori_loop(0, FAR // TILE, turn, 0)

        arrived(q_buf, i, q_recv)
        arrived(g_buf, i, g_recv)
        out, d_query = attend(
            pl.multiple_of(i * TILE, TILE), bias, q_buf[i], g_buf[i], k_win, v_win, k_flip, v_flip, k_sum, v_sum,
            s_buf, p_buf, d_buf,
        )
        o_buf[i] = out
        dq_buf[i] = d_query

        @pl.when(i == h)
        def _():
            start(
                [
                    pltpu.make_async_copy(o_buf.at[i], o_out.at[:, cols(h)], o_recv.at[h]),
                    pltpu.make_async_copy(dq_buf.at[i], dq_out.at[:, cols(h)], dq_recv.at[h]),
                ]
            )

        @pl.when(i != h)
        def _():
            start(
                [
                    remote(o_buf.at[i], o_out.at[:, cols(h)], out_send.at[2 * r], o_recv.at[h], (s, i)),
                    remote(dq_buf.at[i], dq_out.at[:, cols(h)], out_send.at[2 * r + 1], dq_recv.at[h], (s, i)),
                ]
            )

        @pl.when(r == last_far)
        def _():
            lax.fori_loop(0, FAR // TILE, to_part, 0)

            @pl.when(has_prev)
            def _():
                start(far_back)

        @pl.when(r == last_mid)
        def _():
            lax.fori_loop(FAR // TILE, FAR // TILE + 3, to_part, 0)

            @pl.when(has_prev)
            def _():
                start(near_back[0])

        return left // 8

    lax.fori_loop(0, 8, step, code)

    lax.fori_loop(FAR // TILE + 3, FAR // TILE + 5, to_part, 0)

    @pl.when(has_prev)
    def _():
        start(near_back[1])

    @pl.when(has_next)
    def _():
        took(far_back)

    def to_part_far(j, carry):
        full = rows(BACK // TILE - 3 + j)
        k_part[full, :] = (k_sum[full, :] + k_far[rows(j), :].astype(F32)).astype(BF16)
        v_part[full, :] = (v_sum[full, :] + v_far[rows(j), :].astype(F32)).astype(BF16)
        return carry

    lax.fori_loop(0, 3, to_part_far, 0)

    @pl.when(has_prev)
    def _():
        start(near_back[2])

    def total(j, carry):
        full = rows(BACK // TILE + j)
        dk_out[rows(j), :] = ((k_sum[full, :] + k_near[rows(j), :].astype(F32)) * FACTOR).astype(BF16)
        dv_out[rows(j), :] = (v_sum[full, :] + v_near[rows(j), :].astype(F32)).astype(BF16)
        return carry

    for n, (first, size) in enumerate(PIECES[::-1]):

        @pl.when(has_next)
        def _():
            took(near_back[n])

        lax.fori_loop(first // TILE, (first + size) // TILE, total, 0)

    gone(ins)

    @pl.when(has_next)
    def _():
        for copies in near_in + [far_in]:
            gone(copies)

    @pl.when(has_prev)
    def _():
        for copies in near_back + [far_back]:
            gone(copies)

    def finish(r, left):
        i = left % 8
        arrived(o_buf, i, o_recv)
        arrived(dq_buf, i, dq_recv)

        @pl.when(i != h)
        def _():
            for n in range(2):
                pltpu.make_async_copy(o_buf.at[i], o_buf.at[i], out_send.at[2 * r + n]).wait()

        return left // 8

    lax.fori_loop(0, 8, finish, code)


def local(seqs, queries, key_heads, value_heads, output_grad, doc_starts):
    vmem = pl.BlockSpec(memory_space=pltpu.VMEM)
    hbm = pl.BlockSpec(memory_space=pltpu.HBM)
    anywhere = pl.BlockSpec(memory_space=pl.ANY)
    dma = pltpu.SemaphoreType.DMA
    shapes = [jax.ShapeDtypeStruct(queries.shape, BF16)] * 2 + [jax.ShapeDtypeStruct(key_heads.shape, BF16)] * 2
    results = pl.pallas_call(
        functools.partial(kernel, seqs),
        out_shape=shapes,
        in_specs=[hbm] * 5,
        out_specs=[anywhere, anywhere, vmem, vmem],
        scratch_shapes=[pltpu.SMEM(doc_starts.shape, jnp.int32)]
        + [pltpu.VMEM((TILES, TILE, COLS), BF16)] * 4
        + [pltpu.VMEM((ROWS, HEAD), BF16)] * 2
        + [pltpu.VMEM((HEAD, ROWS), BF16)] * 2
        + [pltpu.VMEM((ROWS, HEAD), F32)] * 2
        + [pltpu.VMEM((WIN * TILE, COLS), F32)]
        + [pltpu.VMEM((WIN * TILE, COLS), BF16)] * 2
        + [pltpu.VMEM((BACK, HEAD), BF16)] * 2
        + [pltpu.VMEM((NEAR, HEAD), BF16)] * 2
        + [pltpu.VMEM((FAR, HEAD), BF16)] * 2
        + [dma((14,)), dma((8,)), dma((8,)), dma((16,)), dma((8,)), dma((8,)), dma((16,)), dma((21,))],
        compiler_params=pltpu.CompilerParams(
            collective_id=0, has_side_effects=True, vmem_limit_bytes=48 << 20
        ),
        cost_estimate=pl.CostEstimate(flops=10**10, bytes_accessed=8 << 20, transcendentals=6 << 20),
        name="attention",
    )(*(pltpu.with_memory_space_constraint(a, pltpu.HBM) for a in (doc_starts, queries, key_heads, value_heads, output_grad)))
    return results


def solution(mesh):
    wide = P(("seq", "head"), None)
    narrow = P("seq", "head")
    return jax.shard_map(
        functools.partial(local, mesh.shape["seq"]),
        mesh=mesh,
        in_specs=(wide, narrow, narrow, wide, P()),
        out_specs=(wide, wide, narrow, narrow),
        check_vma=False,
    )
```

time: 89.4 us -> 63 us (0.70)
  the two profiles are of different devices: /device:TPU:1 before, /device:TPU:31 now
where the time goes in v2:
time: 63 us; the launch traced here: 62.9 us
  Pallas kernels  58.9 us (93%)
  local copies, waits for them, and re-layouts  3.35 us (5%)
  between operations  0.64 us (1%)
    pallas_call x1, Pallas kernels, local(): pl.pallas_call(functools.partial(kernel, seqs), out_shape=shapes, in_spec...  58.9 us
    unnamed x4, local copies, waits for them, and re-layouts  3.35 us

profile of v2, /device:TPU:31, one launch (start us, length us, event | category | flops | bytes accessed | tf_op | source)
XLA Modules:
  0.0 62.9 jit_solution(2486831695289321353)
XLA Ops:
  0.6 58.9 %attention.1 = (bf16[128,4096]{1,0:T(8,128)(2,1)S(1)}, bf16[128,4096]{1,0:T(8,128)(2,1)S(1)}, bf16[1024,128]{1,0:T(8,128)(2,1)S(1)}, bf16[1024,128]{1,0:T(8,128)(2,1)S(1)}) custom-call(s32[32]{0:T(128)} %starts_in.1, bf16[128,4096]{1,0:T(8,128)(2,1)} %q_in.1, bf16[1024,128]{1,0:T(8,128)(2,1)} %k_in.1, bf16[1024,128]{1,0:T(8,128)(2,1)} %v_in.1, ...), custom_call_target="tpu_custom_call" | custom-call | flops 10000000000 | bytes 8388608 | tf_op jit(solution)/shard_map/attention/pallas_call | solution.py:425
  59.6 1.0 %copy.13 = bf16[128,4096]{1,0:T(8,128)(2,1)} copy(bf16[128,4096]{1,0:T(8,128)(2,1)S(1)} %get-tuple-element.8) | data formatting | bytes 2097152
  60.5 1.0 %copy.14 = bf16[128,4096]{1,0:T(8,128)(2,1)} copy(bf16[128,4096]{1,0:T(8,128)(2,1)S(1)} %get-tuple-element.9) | data formatting | bytes 2097152
  61.5 0.7 %copy.15 = bf16[1024,128]{1,0:T(8,128)(2,1)} copy(bf16[1024,128]{1,0:T(8,128)(2,1)S(1)} %get-tuple-element.10) | data formatting | bytes 524288
  62.2 0.7 %copy.16 = bf16[1024,128]{1,0:T(8,128)(2,1)} copy(bf16[1024,128]{1,0:T(8,128)(2,1)S(1)} %get-tuple-element.11) | data formatting | bytes 524288

commit v3 on v2

--- a/solution.py
+++ b/solution.py
@@ -35,6 +35,10 @@
     return jnp.dot(a, b, preferred_element_type=F32)
 
 
+def mm_rows(a, b):
+    return lax.dot_general(a, b, (((1,), (1,)), ((), ())), preferred_element_type=F32)
+
+
 def fold(x, op):
     return op(x.reshape(x.shape[0] // 8, 8, x.shape[1]), axis=0)
 
@@ -48,12 +52,12 @@
 
 
 def attend(base, bias, q, g, k_win, v_win, k_flip, v_flip, k_sum, v_sum, s_buf, p_buf, d_buf):
-    q_flip, q_rows = flip(q), stack(q)
+    q_rows = stack(q)
     count = WIN * TILE // CHUNK
     per = CHUNK // TILE
     top = jnp.full((8, COLS), LOW, F32)
     for c in range(count):
-        s = mm(k_win[pl.ds(base + c * CHUNK, CHUNK), :], q_flip)
+        s = mm_rows(k_win[pl.ds(base + c * CHUNK, CHUNK), :], q_rows)
         if c == count - 1:
             key = lax.broadcasted_iota(jnp.int32, (TILE, COLS), 0)
             tok = lax.broadcasted_iota(jnp.int32, (TILE, COLS), 1) % TILE
@@ -72,16 +76,15 @@
     inverse = 1.0 / jnp.sum(total, axis=0, keepdims=True)
     out = (mm(v_flip[:, pl.ds(base, WIN * TILE)], p_buf[...]) * inverse).astype(BF16)
     g_flip = (flip(g).astype(F32) * inverse).astype(BF16)
-    g_rows = stack(flip(g_flip))
     delta = jnp.sum(g_flip.astype(F32) * out.astype(F32), axis=0, keepdims=True)
     for c in range(count):
         rows = slice(c * CHUNK, (c + 1) * CHUNK)
         keys = pl.ds(base + c * CHUNK, CHUNK)
         p = p_buf[rows, :]
         d_prob = mm(v_win[keys, :], g_flip)
-        d_score = (p.astype(F32) * (d_prob - delta)).astype(BF16)
+        d_score = p * (d_prob - delta).astype(BF16)
         d_buf[rows, :] = d_score
-        v_sum[keys, :] += mm(p, g_rows)
+        v_sum[keys, :] += mm_rows(p, g_flip)
         k_sum[keys, :] += mm(d_score, q_rows)
     d_query = (mm(k_flip[:, pl.ds(base, WIN * TILE)], d_buf[...]) * FACTOR).astype(BF16)
     return flip(out), flip(d_query)
@@ -95,14 +98,16 @@
     (6, 4, 5, 2, 3, 0, 1, 7),
     (7, 5, 4, 3, 2, 0, 1, 6),
     (6, 7, 4, 0, 1, 2, 3, 5),
-    (7, 6, 5, 1, 0, 2, 3, 4),
+    (7, 6, 4, 1, 0, 2, 3, 5),
 )
+
 PIECES = ((SHARD - 3 * TILE, 3 * TILE), (SHARD - 5 * TILE, 2 * TILE), (0, 3 * TILE))
 CODE = [sum(tile * 8**n for n, tile in enumerate(row)) for row in ORDER]
 FIRST_MID = [min(n for n, t in enumerate(row) if t < 6) for row in ORDER]
 FIRST_FAR = [min(n for n, t in enumerate(row) if t < 3) for row in ORDER]
 LAST_FAR = [max(n for n, t in enumerate(row) if t < 3) for row in ORDER]
-LAST_MID = [max(n for n, t in enumerate(row) if t < 6) for row in ORDER]
+BACK_PIECES = ((0, 2 * TILE), (2 * TILE, 6 * TILE))
+LAST_MID = [max(n for n, t in enumerate(row) if t < 5) for row in ORDER]
 
 
 def by_head(h, values):
@@ -138,15 +143,11 @@
     for other in others:
         pl.semaphore_signal(barrier, inc=1, device_id=other, device_id_type=MESH)
 
-    @pl.when(has_next)
-    def _():
-        pl.semaphore_signal(barrier, inc=1, device_id=after, device_id_type=MESH)
-
     @pl.when(has_prev)
     def _():
         pl.semaphore_signal(barrier, inc=1, device_id=before, device_id_type=MESH)
 
-    pl.semaphore_wait(barrier, len(others) + jnp.where(has_next, 1, 0) + jnp.where(has_prev, 1, 0))
+    pl.semaphore_wait(barrier, len(others) + jnp.where(has_next, 1, 0))
 
     def cols(head):
         return pl.ds(pl.multiple_of(head * COLS, COLS), COLS)
@@ -191,14 +192,10 @@
 
     @pl.when(has_next)
     def _():
-        start(near_in[0])
+        for copies in near_in:
+            start(copies)
 
     first_ins = regroup(0, 1, 0) + regroup(1, 3, 0)
-
-    @pl.when(has_next)
-    def _():
-        start(near_in[1])
-        start(near_in[2])
 
     ins = regroup(2, 0, 1) + regroup(3, 1, 1) + regroup(4, 3, 1)
     start(
@@ -275,11 +272,11 @@
         [
             remote(
                 part.at[pl.ds(FAR + first, size)], near.at[pl.ds(first, size)], z_send.at[10 + 2 * n + m],
-                z_recv.at[10 + 2 * n + m] if n < 2 else z_recv.at[17 + 2 + m], before,
+                z_recv.at[10 + 2 * n + m], before,
             )
             for m, (part, near, far) in enumerate(parts)
         ]
-        for n, (first, size) in enumerate(PIECES[::-1])
+        for n, (first, size) in enumerate(BACK_PIECES)
     ]
 
     def step(r, left):
@@ -343,7 +340,7 @@
 
         @pl.when(r == last_mid)
         def _():
-            lax.fori_loop(FAR // TILE, FAR // TILE + 3, to_part, 0)
+            lax.fori_loop(FAR // TILE, FAR // TILE + 2, to_part, 0)
 
             @pl.when(has_prev)
             def _():
@@ -353,11 +350,7 @@
 
     lax.fori_loop(0, 8, step, code)
 
-    lax.fori_loop(FAR // TILE + 3, FAR // TILE + 5, to_part, 0)
-
-    @pl.when(has_prev)
-    def _():
-        start(near_back[1])
+    lax.fori_loop(FAR // TILE + 2, FAR // TILE + 5, to_part, 0)
 
     @pl.when(has_next)
     def _():
@@ -373,7 +366,7 @@
 
     @pl.when(has_prev)
     def _():
-        start(near_back[2])
+        start(near_back[1])
 
     def total(j, carry):
         full = rows(BACK // TILE + j)
@@ -381,7 +374,7 @@
         dv_out[rows(j), :] = (v_sum[full, :] + v_near[rows(j), :].astype(F32)).astype(BF16)
         return carry
 
-    for n, (first, size) in enumerate(PIECES[::-1]):
+    for n, (first, size) in enumerate(BACK_PIECES):
 
         @pl.when(has_next)
         def _():
@@ -437,7 +430,7 @@
         + [pltpu.VMEM((BACK, HEAD), BF16)] * 2
         + [pltpu.VMEM((NEAR, HEAD), BF16)] * 2
         + [pltpu.VMEM((FAR, HEAD), BF16)] * 2
-        + [dma((14,)), dma((8,)), dma((8,)), dma((16,)), dma((8,)), dma((8,)), dma((16,)), dma((21,))],
+        + [dma((14,)), dma((8,)), dma((8,)), dma((16,)), dma((8,)), dma((8,)), dma((14,)), dma((19,))],
         compiler_params=pltpu.CompilerParams(
             collective_id=0, has_side_effects=True, vmem_limit_bytes=48 << 20
         ),

time: 63 us -> 62.5 us (level)
  no operation moved by 1% of the time
where the time goes in v3:
time: 62.5 us; the launch traced here: 62.4 us
  Pallas kernels  58.4 us (93%)
  local copies, waits for them, and re-layouts  3.35 us (5%)
  between operations  0.64 us (1%)
    pallas_call x1, Pallas kernels, local(): pl.pallas_call(functools.partial(kernel, seqs), out_shape=shapes, in_spec...  58.4 us
    unnamed x4, local copies, waits for them, and re-layouts  3.35 us

profile of v3, /device:TPU:31, one launch (start us, length us, event | category | flops | bytes accessed | tf_op | source)
XLA Modules:
  0.0 62.4 jit_solution(9018510797325259646)
XLA Ops:
  0.6 58.4 %attention.1 = (bf16[128,4096]{1,0:T(8,128)(2,1)S(1)}, bf16[128,4096]{1,0:T(8,128)(2,1)S(1)}, bf16[1024,128]{1,0:T(8,128)(2,1)S(1)}, bf16[1024,128]{1,0:T(8,128)(2,1)S(1)}) custom-call(s32[32]{0:T(128)} %starts_in.1, bf16[128,4096]{1,0:T(8,128)(2,1)} %q_in.1, bf16[1024,128]{1,0:T(8,128)(2,1)} %k_in.1, bf16[1024,128]{1,0:T(8,128)(2,1)} %v_in.1, ...), custom_call_target="tpu_custom_call" | custom-call | flops 10000000000 | bytes 8388608 | tf_op jit(solution)/shard_map/attention/pallas_call | solution.py:418
  59.1 1.0 %copy.13 = bf16[128,4096]{1,0:T(8,128)(2,1)} copy(bf16[128,4096]{1,0:T(8,128)(2,1)S(1)} %get-tuple-element.8) | data formatting | bytes 2097152
  60.0 1.0 %copy.14 = bf16[128,4096]{1,0:T(8,128)(2,1)} copy(bf16[128,4096]{1,0:T(8,128)(2,1)S(1)} %get-tuple-element.9) | data formatting | bytes 2097152
  61.0 0.7 %copy.15 = bf16[1024,128]{1,0:T(8,128)(2,1)} copy(bf16[1024,128]{1,0:T(8,128)(2,1)S(1)} %get-tuple-element.10) | data formatting | bytes 524288
  61.7 0.7 %copy.16 = bf16[1024,128]{1,0:T(8,128)(2,1)} copy(bf16[1024,128]{1,0:T(8,128)(2,1)S(1)} %get-tuple-element.11) | data formatting | bytes 524288

commit v4 on v3

--- a/solution.py
+++ b/solution.py
@@ -101,9 +101,9 @@
     (7, 6, 4, 1, 0, 2, 3, 5),
 )
 
-PIECES = ((SHARD - 3 * TILE, 3 * TILE), (SHARD - 5 * TILE, 2 * TILE), (0, 3 * TILE))
+PIECES = ((SHARD - 3 * TILE, 3 * TILE), (SHARD - 6 * TILE, 3 * TILE), (0, 2 * TILE))
 CODE = [sum(tile * 8**n for n, tile in enumerate(row)) for row in ORDER]
-FIRST_MID = [min(n for n, t in enumerate(row) if t < 6) for row in ORDER]
+FIRST_MID = [min(n for n, t in enumerate(row) if t < 5) for row in ORDER]
 FIRST_FAR = [min(n for n, t in enumerate(row) if t < 3) for row in ORDER]
 LAST_FAR = [max(n for n, t in enumerate(row) if t < 3) for row in ORDER]
 BACK_PIECES = ((0, 2 * TILE), (2 * TILE, 6 * TILE))

time: 62.5 us -> 60.9 us (0.974)
  Pallas kernels: 58.4 us -> 56.8 us
    pallas_call x1, Pallas kernels: 58.4 us -> 56.8 us  [local(): pl.pallas_call(functools.partial(kernel, seqs), out_shape=shapes, in_spec...]
where the time goes in v4:
time: 60.9 us; the launch traced here: 60.8 us
  Pallas kernels  56.8 us (93%)
  local copies, waits for them, and re-layouts  3.35 us (6%)
  between operations  0.64 us (1%)
    pallas_call x1, Pallas kernels, local(): pl.pallas_call(functools.partial(kernel, seqs), out_shape=shapes, in_spec...  56.8 us
    unnamed x4, local copies, waits for them, and re-layouts  3.35 us

profile of v4, /device:TPU:31, one launch (start us, length us, event | category | flops | bytes accessed | tf_op | source)
XLA Modules:
  0.0 60.8 jit_solution(458764115063276680)
XLA Ops:
  0.6 56.8 %attention.1 = (bf16[128,4096]{1,0:T(8,128)(2,1)S(1)}, bf16[128,4096]{1,0:T(8,128)(2,1)S(1)}, bf16[1024,128]{1,0:T(8,128)(2,1)S(1)}, bf16[1024,128]{1,0:T(8,128)(2,1)S(1)}) custom-call(s32[32]{0:T(128)} %starts_in.1, bf16[128,4096]{1,0:T(8,128)(2,1)} %q_in.1, bf16[1024,128]{1,0:T(8,128)(2,1)} %k_in.1, bf16[1024,128]{1,0:T(8,128)(2,1)} %v_in.1, ...), custom_call_target="tpu_custom_call" | custom-call | flops 10000000000 | bytes 8388608 | tf_op jit(solution)/shard_map/attention/pallas_call | solution.py:418
  57.4 1.0 %copy.13 = bf16[128,4096]{1,0:T(8,128)(2,1)} copy(bf16[128,4096]{1,0:T(8,128)(2,1)S(1)} %get-tuple-element.8) | data formatting | bytes 2097152
  58.4 1.0 %copy.14 = bf16[128,4096]{1,0:T(8,128)(2,1)} copy(bf16[128,4096]{1,0:T(8,128)(2,1)S(1)} %get-tuple-element.9) | data formatting | bytes 2097152
  59.4 0.7 %copy.15 = bf16[1024,128]{1,0:T(8,128)(2,1)} copy(bf16[1024,128]{1,0:T(8,128)(2,1)S(1)} %get-tuple-element.10) | data formatting | bytes 524288
  60.1 0.7 %copy.16 = bf16[1024,128]{1,0:T(8,128)(2,1)} copy(bf16[1024,128]{1,0:T(8,128)(2,1)S(1)} %get-tuple-element.11) | data formatting | bytes 524288
